TPU v7x, 32 devices: a whole 2x2x4 slice. The times are simulated.
32 devices in a mesh: groups: 2 (over x), face: 8 (over z, y), tile: 2 (over core).
Axes of the slice: x: 2, y: 2, z: 4, core: 2. Of those that a mesh axis runs over, the one named last changes fastest.
Arguments:
- fields: float32 [32, 64, 128, 128], P(('groups', 'face'), None, 'tile'), parts along dimension 0, may hold values from -8 to 8
- cotangent: float32 [32, 64, 128, 128], P(('groups', 'face'), None, 'tile'), parts along dimension 0, may hold values from -0.125 to 0.125
- first_kernel: float32 [64, 64, 3, 3], replicated, may hold values from -0.25 to 0.25
- second_kernel: float32 [64, 64, 3, 3], replicated, may hold values from -0.25 to 0.25
- coarse_kernel: float32 [64, 64, 3, 3], replicated, may hold values from -0.25 to 0.25
- slot_faces: int32 [16], replicated, may hold values from -1 to 11, as said below
- edge_table: int32 [16, 4, 2], replicated, may hold values from 0 to 15, as said below
- corner_table: int32 [16, 4, 3], replicated, may hold values from 0 to 15, as said below
Outputs:
- section_output: float32 [32, 64, 128, 128], P(('groups', 'face'), None, 'tile'), parts along dimension 0
- grad_first: float32 [128, 64, 3, 3], P('groups'), parts along dimension 0
- grad_second: float32 [128, 64, 3, 3], P('groups'), parts along dimension 0
- grad_coarse: float32 [128, 64, 3, 3], P('groups'), parts along dimension 0
There are 2 independent parts, one for each index of `groups`. A program takes and returns all parts, laid end to end along the dimension named above; an argument that names none is the same for every part. Nothing has to cross between parts.
Inputs may be any that keep to these rules, and one draw needn't show every extreme that they name: `slot_faces`: each face 0 to 11 stands in exactly one slot; the other slots hold -1. `edge_table`: for an occupied slot the entries follow the HEALPix base tessellation under the slot map; an empty slot names itself and its own side. The relation is symmetric: if side s of slot q names side t of slot p, then side t of p names side s of q. `corner_table`: entry [q, k, 2] is 1 where a fourth face meets diagonally at corner k, else 0 and the entry names slot q and corner k itself; empty slots name themselves. The relation is symmetric: if corner k of q names corner m of p, then corner m of p names corner k of q.
All inputs are finite; a program needn't handle non-finite values.
Results may differ from a plain program's by a relative error of at most 0.0003.
Values sent between devices are 32-bit elements; how exact they have to be, the bound alone decides.
A program may use at most 256 MiB of HBM per device.

v0:
```python
from functools import partial

import jax
import jax.numpy as jnp
from jax import lax
from jax.sharding import PartitionSpec as P

BLOCK = 4


def convolve(padded, kernel):
    return lax.conv_general_dilated(
        padded, kernel, (1, 1), "VALID", precision=lax.Precision.HIGHEST
    )


def activate(values):
    return jax.nn.gelu(values, approximate=False)


def rim_pieces(tile_field):
    last_row = tile_field.shape[2] - 1
    last_col = tile_field.shape[3] - 1
    columns = jnp.stack([tile_field[:, :, :, 0], tile_field[:, :, :, last_col]], axis=1)[None]
    borders = jnp.stack([tile_field[:, :, 0, :], tile_field[:, :, last_row, :]], axis=1)[None]
    return (columns, borders)


def whole_pieces(gathered):
    columns = jnp.stack([gathered[..., 0], gathered[..., -1]], axis=2)
    borders = jnp.stack([gathered[..., 0, :], gathered[..., -1, :]], axis=2)
    return (columns, borders)


def fine_gather(tile_field):
    columns, borders = rim_pieces(tile_field)
    return (
        lax.all_gather(columns, ("face", "tile"), axis=0, tiled=True),
        lax.all_gather(borders, ("face", "tile"), axis=0, tiled=True),
    )


def fetch_lines(
    columns_all, borders_all, face_index, tile_index, face_count, tile_count, my_edges, my_corners
):
    slots_dev = columns_all.shape[1]
    channels = columns_all.shape[3]
    tile_rows = columns_all.shape[4]
    length = borders_all.shape[-1]
    cols_all = columns_all.reshape(face_count, tile_count, slots_dev, 2, channels, tile_rows)
    bord_all = borders_all.reshape(face_count, tile_count, slots_dev, 2, channels, length)
    near_slot = my_edges[:, :, 0]
    near_side = my_edges[:, :, 1]
    near_face = near_slot // slots_dev
    near_local = near_slot % slots_dev
    col_pick = jnp.where(near_side == 1, 1, 0)
    col_lines = cols_all[near_face, :, near_local, col_pick]
    col_lines = col_lines.transpose(0, 1, 3, 2, 4).reshape(
        slots_dev, 4, channels, tile_count * tile_rows
    )
    row_tile = jnp.where(near_side == 0, 0, tile_count - 1)
    row_pick = jnp.where(near_side == 0, 0, 1)
    row_lines = bord_all[near_face, row_tile, near_local, row_pick]
    halo_lines = jnp.where((near_side % 2 == 1)[:, :, None, None], col_lines, row_lines)
    corner_slot = my_corners[:, :, 0]
    corner_kind = my_corners[:, :, 1]
    corner_face = corner_slot // slots_dev
    corner_local = corner_slot % slots_dev
    corner_tile = jnp.where(corner_kind < 2, 0, tile_count - 1)
    corner_row = jnp.where(corner_kind < 2, 0, 1)
    corner_col = jnp.where((corner_kind == 0) | (corner_kind == 3), 0, length - 1)
    picked = bord_all[corner_face, corner_tile, corner_local, corner_row, :, corner_col]
    above_tile = bord_all[face_index, jnp.maximum(tile_index - 1, 0), :, 1]
    below_tile = bord_all[face_index, jnp.minimum(tile_index + 1, tile_count - 1), :, 0]
    return (halo_lines, picked, above_tile, below_tile)


def assemble(tile_field, pieces, tile_index, tile_count, my_corners):
    halo_lines, picked, above_tile, below_tile = pieces
    tile_rows = tile_field.shape[2]
    corner_flag = my_corners[:, :, 2]
    south_east = halo_lines[:, 0]
    north_east = halo_lines[:, 1]
    north_west = halo_lines[:, 2]
    south_west = halo_lines[:, 3]
    averaged = jnp.stack(
        [
            0.5 * (south_east[..., 0] + south_west[..., 0]),
            0.5 * (south_east[..., -1] + north_east[..., 0]),
            0.5 * (north_west[..., -1] + north_east[..., -1]),
            0.5 * (north_west[..., 0] + south_west[..., -1]),
        ],
        axis=1,
    )
    corners = jnp.where((corner_flag == 1)[:, :, None], picked, averaged)
    west_line = jnp.concatenate(
        [corners[:, 0, :, None], south_west, corners[:, 3, :, None]], axis=-1
    )
    east_line = jnp.concatenate(
        [corners[:, 1, :, None], north_east, corners[:, 2, :, None]], axis=-1
    )
    west_part = lax.dynamic_slice_in_dim(west_line, tile_index * tile_rows, tile_rows + 2, axis=2)
    east_part = lax.dynamic_slice_in_dim(east_line, tile_index * tile_rows, tile_rows + 2, axis=2)
    above_row = jnp.where(tile_index == 0, south_east, above_tile)
    below_row = jnp.where(tile_index == tile_count - 1, north_west, below_tile)
    top_row = jnp.concatenate([west_part[..., :1], above_row, east_part[..., :1]], axis=-1)
    bottom = jnp.concatenate([west_part[..., -1:], below_row, east_part[..., -1:]], axis=-1)
    middle = jnp.concatenate(
        [west_part[..., 1:-1, None], tile_field, east_part[..., 1:-1, None]], axis=-1
    )
    return jnp.concatenate([top_row[:, :, None], middle, bottom[:, :, None]], axis=2)


def framed_tile(
    tile_field,
    columns_all,
    borders_all,
    face_index,
    tile_index,
    face_count,
    tile_count,
    my_edges,
    my_corners,
):
    pieces = fetch_lines(
        columns_all,
        borders_all,
        face_index,
        tile_index,
        face_count,
        tile_count,
        my_edges,
        my_corners,
    )
    return assemble(tile_field, pieces, tile_index, tile_count, my_corners)


def local(
    fields,
    cotangent,
    first_kernel,
    second_kernel,
    coarse_kernel,
    slot_faces,
    edge_table,
    corner_table,
):
    face_index = lax.axis_index("face")
    tile_index = lax.axis_index("tile")
    face_count = lax.axis_size("face")
    tile_count = lax.axis_size("tile")
    slots_dev = fields.shape[0]
    my_slots = face_index * slots_dev + jnp.arange(slots_dev, dtype=jnp.int32)
    my_edges = edge_table[my_slots]
    my_corners = corner_table[my_slots]
    occupied = (slot_faces[my_slots] >= 0).astype(jnp.float32)[:, None, None, None]
    framer = partial(
        framed_tile,
        face_index=face_index,
        tile_index=tile_index,
        face_count=face_count,
        tile_count=tile_count,
        my_edges=my_edges,
        my_corners=my_corners,
    )
    columns_in, borders_in = fine_gather(fields)
    padded_in = framer(fields, columns_in, borders_in)
    first_act = convolve(padded_in, first_kernel)
    hidden, hidden_pull = jax.vjp(activate, first_act)
    columns_mid, borders_mid = fine_gather(hidden)
    padded_mid, frame_pull = jax.vjp(framer, hidden, columns_mid, borders_mid)
    second_act, second_pull = jax.vjp(convolve, padded_mid, second_kernel)
    features, features_pull = jax.vjp(activate, second_act)
    channels = features.shape[1]
    tile_rows = features.shape[2]
    length = features.shape[3]
    coarse = features.reshape(
        slots_dev, channels, tile_rows // BLOCK, BLOCK, length // BLOCK, BLOCK
    ).mean(axis=(3, 5))
    everything = lax.all_gather(coarse[None], ("face", "tile"), axis=0, tiled=True)

    def coarse_frame(tile_field, gathered):
        columns_all, borders_all = whole_pieces(gathered)
        return framer(tile_field, columns_all, borders_all)

    padded_low, low_pull = jax.vjp(coarse_frame, coarse, everything)
    coarse_act, coarse_pull = jax.vjp(convolve, padded_low, coarse_kernel)
    bottleneck, bottleneck_pull = jax.vjp(activate, coarse_act)
    widened = jnp.repeat(jnp.repeat(bottleneck, BLOCK, axis=2), BLOCK, axis=3)
    section_output = (features + widened) * occupied
    masked = cotangent * occupied
    grad_bottleneck = masked.reshape(
        slots_dev, channels, tile_rows // BLOCK, BLOCK, length // BLOCK, BLOCK
    ).sum(axis=(3, 5))
    (grad_coarse_act,) = bottleneck_pull(grad_bottleneck)
    grad_padded_low, grad_coarse = coarse_pull(grad_coarse_act)
    grad_local, grad_everything = low_pull(grad_padded_low)
    returned = lax.psum_scatter(grad_everything, ("face", "tile"), scatter_dimension=0, tiled=True)
    grad_low = grad_local + returned[0]
    grad_features = masked + jnp.repeat(jnp.repeat(grad_low, BLOCK, axis=2), BLOCK, axis=3) / (
        BLOCK * BLOCK
    )
    (grad_second_act,) = features_pull(grad_features)
    grad_padded_mid, grad_second = second_pull(grad_second_act)
    grad_hidden_local, grad_columns_mid, grad_borders_mid = frame_pull(grad_padded_mid)
    back_columns_mid, back_borders_mid = (
        lax.psum_scatter(grad_columns_mid, ("face", "tile"), scatter_dimension=0, tiled=True),
        lax.psum_scatter(grad_borders_mid, ("face", "tile"), scatter_dimension=0, tiled=True),
    )
    (spread_mid,) = jax.vjp(rim_pieces, hidden)[1]((back_columns_mid, back_borders_mid))
    grad_hidden = grad_hidden_local + spread_mid
    (grad_first_act,) = hidden_pull(grad_hidden)
    (grad_first,) = jax.vjp(partial(convolve, padded_in), first_kernel)[1](grad_first_act)
    grad_first, grad_second, grad_coarse = lax.psum(
        (grad_first, grad_second, grad_coarse), ("face", "tile")
    )
    return (section_output, grad_first, grad_second, grad_coarse)


def solution(mesh):
    in_specs = (
        P(("groups", "face"), None, "tile", None),
        P(("groups", "face"), None, "tile", None),
        P(),
        P(),
        P(),
        P(),
        P(),
        P(),
    )
    out_specs = (
        P(("groups", "face"), None, "tile", None),
        P("groups", None, None, None),
        P("groups", None, None, None),
        P("groups", None, None, None),
    )
    return jax.shard_map(local, mesh=mesh, in_specs=in_specs, out_specs=out_specs, check_vma=False)
```

profile of v0, /device:TPU:0, one launch (start us, length us, event | category | flops | bytes accessed | tf_op | source)
XLA Modules:
  0.0 1486.7 jit_solution(15681777491783752644)
XLA Ops:
  36.6 29.7 %all-gather.13.cloned.1.call-done = f32[32,2,64,64]{3,2,0,1:T(8,128)} async-done(((f32[2,2,64,64]{3,2,0,1:T(8,128)}), f32[32,2,64,64]{3,2,0,1:T(8,128)}) %all-gather.13.cloned.1.call-update) | async-done | bytes 1048592 | tf_op jit(solution)/shard_map/all_gather | solution.py:38
  68.8 40.6 %all-gather.11.cloned.1.call-done = f32[32,2,64,128]{3,2,0,1:T(8,128)} async-done(((f32[2,2,64,128]{3,2,0,1:T(8,128)}), f32[32,2,64,128]{3,2,0,1:T(8,128)}) %all-gather.11.cloned.1.call-update) | async-done | bytes 2097168 | tf_op jit(solution)/shard_map/all_gather | solution.py:39
  119.7 28.1 %fusion.205 = f32[64,66,2,130]{0,2,3,1:T(2,128)S(1)} fusion(f32[2,64,1,130]{1,0,3,2:T(2,128)S(1)} %maximum_bitcast_fusion.1, f32[2,64,64,1]{1,0,3,2:T(2,128)S(1)} %slice_bitcast_fusion.18, f32[2,64,64,128]{1,0,3,2:T(2,128)} %copy.868, f32[2,64,64,1]{1,0,3,2:T(2,128)S(1)} %slice_bitcast_fusion.19, f32[2,64,1,130]{1,0,3,2:T(2,128)S(1)} %maximum_bitcast_fusion), kind=kLoop, calls=%fused_computation.478 | loop fusion | flops 4392960 | bytes 8785920 | tf_op jit(solution)/shard_map/concatenate | solution.py:111
  152.5 104.1 %select_multiply_fusion.1 = (f32[64,16,17,64]{3,1,2,0:T(8,128)}, f32[64,16,17,64]{3,1,2,0:T(8,128)}, f32[64,16,17,64]{3,1,2,0:T(8,128)}, f32[64,16,17,64]{3,1,2,0:T(8,128)}) fusion(pred[16,17]{0,1:T(8,128)(4,1)S(1)} %copy-done.66, f32[64,64,3,3]{1,0,3,2:T(8,128)S(1)} %copy-done.62, f32[64,66,2,7,2]{0,3,2,4,1:T(8,128)S(1)} %slice.480, ...), kind=kOutput, calls=%fused_computation.66 | convolution fusion | flops 7777011712 | bytes 23042320 | tf_op jit(solution)/shard_map/conv_general_dilated | solution.py:12
  264.6 9.7 copy.1083
  280.9 38.1 %all-gather.17.cloned.1.call-done = f32[32,2,64,64]{3,2,1,0:T(8,128)} async-done(((f32[2,2,64,64]{3,2,1,0:T(8,128)}), f32[32,2,64,64]{3,2,1,0:T(8,128)}) %all-gather.17.cloned.1.call-update) | async-done | bytes 1048592 | tf_op jit(solution)/shard_map/all_gather | solution.py:38
  321.4 49.6 %all-gather.15.cloned.1.call-done = f32[32,2,64,128]{2,3,0,1:T(8,128)} async-done(((f32[2,2,64,128]{2,3,0,1:T(8,128)}), f32[32,2,64,128]{2,3,0,1:T(8,128)}) %all-gather.15.cloned.1.call-update) | async-done | bytes 2097168 | tf_op jit(solution)/shard_map/all_gather | solution.py:39
  382.2 28.1 %fusion.204 = f32[64,66,2,130]{0,2,3,1:T(2,128)S(1)} fusion(f32[2,64,1,130]{1,0,3,2:T(2,128)S(1)} %maximum_bitcast_fusion.3, f32[2,64,64,1]{1,0,3,2:T(2,128)S(1)} %slice_bitcast_fusion.14, f32[2,64,64,128]{1,0,3,2:T(2,128)} %bitcast.494, f32[2,64,64,1]{1,0,3,2:T(2,128)S(1)} %slice_bitcast_fusion.15, f32[2,64,1,130]{1,0,3,2:T(2,128)S(1)} %maximum_bitcast_fusion.2), kind=kLoop, calls=%fused_computation.477 | loop fusion | flops 4392960 | bytes 8785920 | tf_op jit(solution)/shard_map/jvp()/concatenate | solution.py:111
  414.8 88.7 %select_multiply_fusion = (f32[64,16,17,64]{3,1,2,0:T(8,128)}, f32[64,16,17,64]{3,1,2,0:T(8,128)}, f32[64,16,17,64]{3,1,2,0:T(8,128)S(1)}, f32[64,16,17,64]{3,1,2,0:T(8,128)}) fusion(pred[16,17]{0,1:T(8,128)(4,1)S(1)} %copy-done.66, f32[64,64,3,3]{1,0,3,2:T(8,128)S(1)} %copy-done, f32[64,66,2,7,2]{0,3,2,4,1:T(8,128)S(1)} %slice.510, ...), kind=kOutput, calls=%fused_computation.65 | convolution fusion | flops 7777011712 | bytes 23042320 | tf_op jit(solution)/shard_map/jvp()/conv_general_dilated | solution.py:12
  509.7 12.2 fusion.174
  522.0 11.4 copy.893
  551.5 63.4 %all-gather.19.cloned.1.call-done = f32[32,64,16,32]{1,3,2,0:T(8,128)} async-done(((f32[2,64,16,32]{1,3,2,0:T(8,128)}), f32[32,64,16,32]{1,3,2,0:T(8,128)}) %all-gather.19.cloned.1.call-update) | async-done | bytes 4194320 | tf_op jit(solution)/shard_map/all_gather | solution.py:180
  648.4 10.5 broadcast_multiply_fusion
  697.9 9.3 copy.1004
  823.9 12.2 fusion.35
  853.1 9.7 select_maximum_fusion.2
  862.8 11.3 copy.953
  874.0 48.8 %broadcast_select_fusion = f32[66,16,17,64]{3,1,2,0:T(8,128)S(1)} fusion(pred[16,17]{0,1:T(8,128)(4,1)S(1)} %copy-done.65, f32[64,64,3,3]{1,0,3,2:T(8,128)S(1)} %copy-done, f32[64,64,2,8,19]{0,3,2,4,1:T(8,128)} %copy.953), kind=kOutput, calls=%fused_computation.73 | convolution fusion | flops 7701891072 | bytes 9724176 | tf_op jit(solution)/shard_map/transpose(jvp())/conv_general_dilated | solution.py:12
  926.5 11.4 copy.954
  947.0 11.2 copy.1018
  1022.5 165.6 %fusion.193 = f32[64,64,3,3]{0,1,3,2:T(8,128)} fusion(f32[2,64,64,128]{1,0,3,2:T(2,128)} %copy.978, f32[2,64,1,130]{1,0,3,2:T(2,128)S(1)} %copy-done.20, f32[2,64,64,1]{1,0,3,2:T(2,128)S(1)} %copy-done.32, f32[2,64,64,128]{1,0,3,2:T(2,128)} %bitcast.495, f32[2,64,64,1]{1,0,3,2:T(2,128)S(1)} %copy-done.30, f32[2,64,1,130]{1,0,3,2:T(2,128)S(1)} %copy-done.18), kind=kOutput, calls=%fused_computation.475 | convolution fusion | flops 7252150272 | bytes 8734720 | tf_op jit(solution)/shard_map/transpose(jvp())/conv_general_dilated | solution.py:12
  1195.6 13.5 fusion.31
  1217.6 165.2 %fusion.192 = f32[64,64,3,3]{0,1,3,2:T(8,128)} fusion(f32[2,64,64,128]{1,0,3,2:T(2,128)} %copy.977, f32[2,64,1,130]{1,0,3,2:T(2,128)S(1)} %copy-done.16, f32[2,64,64,1]{1,0,3,2:T(2,128)S(1)} %copy-done.28, f32[2,64,64,128]{1,0,3,2:T(2,128)} %copy.868, f32[2,64,64,1]{1,0,3,2:T(2,128)S(1)} %copy-done.26, f32[2,64,1,130]{1,0,3,2:T(2,128)S(1)} %copy-done.14), kind=kOutput, calls=%fused_computation.474 | convolution fusion | flops 7252150272 | bytes 8734720 | tf_op jit(solution)/shard_map/transpose(jvp())/conv_general_dilated | solution.py:12
  1382.8 91.7 %all-reduce.49.cloned.1.call-done = (f32[64,64,3,3]{0,1,3,2:T(8,128)}, f32[64,64,3,3]{0,1,3,2:T(8,128)}, f32[64,64,3,3]{0,1,3,2:T(8,128)}) async-done(((f32[64,64,3,3]{0,1,3,2:T(8,128)}, f32[64,64,3,3]{0,1,3,2:T(8,128)}, f32[64,64,3,3]{0,1,3,2:T(8,128)}), (f32[64,64,3,3]{0,1,3,2:T(8,128)}, f32[64,64,3,3]{0,1,3,2:T(8,128)}, f32[64,64,3,3]{0,1,3,2:T(8,128)})) %all-reduce.49.cloned.1.call-update) | async-done | bytes 442384 | tf_op jit(solution)/shard_map/psum | solution.py:214
  (414 shorter events, 406.6 us)
Async XLA Ops:
  7.2 407.6 %copy-start = (f32[64,64,3,3]{1,0,3,2:T(8,128)S(1)}, f32[64,64,3,3]{1,0,3,2:T(8,128)}, u32[]{:S(2)}) copy-start(f32[64,64,3,3]{1,0,3,2:T(8,128)} %param.11) | copy-start | bytes 442372
  7.2 59.1 %all-gather.13.cloned.1.call-start = ((), (), s32[]{:S(2)}) async-start(), calls=%async_computation.7 | async-start | bytes 2228224 | tf_op jit(solution)/shard_map/all_gather | solution.py:38
  22.1 87.2 %all-gather.11.cloned.1.call-start = ((), (), s32[]{:S(2)}) async-start(), calls=%async_computation.6 | async-start | bytes 2228224 | tf_op jit(solution)/shard_map/all_gather | solution.py:39
  24.1 294.9 %all-gather.17.cloned.1.call-start = ((), (), s32[]{:S(2)}) async-start(), calls=%async_computation.9 | async-start | bytes 2228224 | tf_op jit(solution)/shard_map/all_gather | solution.py:38
  33.5 347.3 %copy-start.46 = (pred[2,4]{0,1:T(4,128)(4,1)}, pred[2,4]{0,1:T(4,128)(4,1)S(1)}, u32[]{:S(2)}) copy-start(pred[2,4]{0,1:T(4,128)(4,1)S(1)} %copy.858) | copy-start | bytes 28
  33.8 344.2 %copy-start.21 = (s32[8]{0:T(128)}, s32[8]{0:T(128)S(1)}, u32[]{:S(2)}) copy-start(s32[8]{0:T(128)S(1)} %reshape.664) | copy-start | bytes 100
  34.8 346.6 %copy-start.49 = (pred[2,4,1]{0,1,2:T(4,128)(4,1)}, pred[2,4,1]{0,1,2:T(4,128)(4,1)S(1)}, u32[]{:S(2)}) copy-start(pred[2,4,1]{0,1,2:T(4,128)(4,1)S(1)} %copy.984) | copy-start | bytes 28
  35.7 283.3 %copy-start.23 = (s32[8]{0:T(128)}, s32[8]{0:T(128)S(1)}, u32[]{:S(2)}) copy-start(s32[8]{0:T(128)S(1)} %reshape.658) | copy-start | bytes 100
  278.7 92.3 %all-gather.15.cloned.1.call-start = ((), (), s32[]{:S(2)}) async-start(), calls=%async_computation.8 | async-start | bytes 4456448 | tf_op jit(solution)/shard_map/all_gather | solution.py:39
  280.8 334.1 %all-gather.19.cloned.1.call-start = ((), (), s32[]{:S(2)}) async-start(), calls=%async_computation.10 | async-start | bytes 8912896 | tf_op jit(solution)/shard_map/all_gather | solution.py:180
  540.2 81.4 %copy-start.7 = (f32[2,64,16,32]{1,0,2,3:T(2,128)}, f32[2,64,16,32]{1,0,2,3:T(2,128)S(1)}, u32[]{:S(2)}) copy-start(f32[2,64,16,32]{1,0,2,3:T(2,128)S(1)} %copy_multiply_fusion) | copy-start | bytes 786436
  541.3 264.3 %reduce-scatter.4.cloned.1.call-start = ((), (), s32[]{:S(2)}) async-start(), calls=%async_computation.3 | async-start | bytes 8912896 | tf_op jit(solution)/shard_map/reduce_scatter | solution.py:198
  542.2 138.7 %copy-start.39 = (s32[8]{0:T(128)}, s32[8]{0:T(128)S(1)}, u32[]{:S(2)}) copy-start(s32[8]{0:T(128)S(1)} %reshape.726) | copy-start | bytes 100
  542.3 136.4 %copy-start.37 = (s32[8]{0:T(128)}, s32[8]{0:T(128)S(1)}, u32[]{:S(2)}) copy-start(s32[8]{0:T(128)S(1)} %reshape.714) | copy-start | bytes 100
  542.5 76.6 %copy-start.24 = (s32[8]{0:T(128)S(1)}, s32[8]{0:T(128)}, u32[]{:S(2)}) copy-start(s32[8]{0:T(128)} %copy-done.23) | copy-start | bytes 100
  542.5 77.2 %copy-start.22 = (s32[8]{0:T(128)S(1)}, s32[8]{0:T(128)}, u32[]{:S(2)}) copy-start(s32[8]{0:T(128)} %copy-done.21) | copy-start | bytes 100
  542.5 78.4 %copy-start.47 = (pred[2,4]{0,1:T(4,128)(4,1)S(1)}, pred[2,4]{0,1:T(4,128)(4,1)}, u32[]{:S(2)}) copy-start(pred[2,4]{0,1:T(4,128)(4,1)} %copy-done.46) | copy-start | bytes 28
  542.5 78.7 %copy-start.50 = (pred[2,4,1]{0,1,2:T(4,128)(4,1)S(1)}, pred[2,4,1]{0,1,2:T(4,128)(4,1)}, u32[]{:S(2)}) copy-start(pred[2,4,1]{0,1,2:T(4,128)(4,1)} %copy-done.49) | copy-start | bytes 28
  551.5 72.0 %copy-start.63 = (f32[64,64,3,3]{1,0,3,2:T(8,128)S(1)}, f32[64,64,3,3]{1,0,3,2:T(8,128)}, u32[]{:S(2)}) copy-start(f32[64,64,3,3]{1,0,3,2:T(8,128)} %param.12) | copy-start | bytes 442372
  551.5 72.0 %copy-start.68 = (pred[16,5]{0,1:T(8,128)(4,1)S(1)}, pred[16,5]{0,1:T(8,128)(4,1)}, u32[]{:S(2)}) copy-start(pred[16,5]{0,1:T(8,128)(4,1)} %constant.349) | copy-start | bytes 244
  685.8 502.3 %reduce-scatter.8.cloned.1.call-start = ((), (), s32[]{:S(2)}) async-start(), calls=%async_computation.5 | async-start | bytes 2228224 | tf_op jit(solution)/shard_map/reduce_scatter | solution.py:207
  983.0 211.7 %reduce-scatter.6.cloned.1.call-start = ((), (), s32[]{:S(2)}) async-start(), calls=%async_computation.4 | async-start | bytes 2228224 | tf_op jit(solution)/shard_map/reduce_scatter | solution.py:208
  1022.4 452.1 %all-reduce.49.cloned.1.call-start = ((), (), s32[]{:S(2)}) async-start(), calls=%async_computation.11 | async-start | bytes 1769472 | tf_op jit(solution)/shard_map/psum | solution.py:214
  1217.6 262.4 %copy-start.1 = (f32[64,64,3,3]{1,0,3,2:T(8,128)S(1)}, f32[64,64,3,3]{1,0,3,2:T(8,128)}, u32[]{:S(2)}) copy-start(f32[64,64,3,3]{1,0,3,2:T(8,128)} %param.11) | copy-start | bytes 442372
  (54 other events, 666.2 us)
Sparse Core Ops, SparseCore 0:
  22.2 44.0 all-gather.12
  69.1 40.1 all-gather.10
  278.8 40.1 all-gather.16
  321.6 49.3 all-gather.14
  541.4 73.3 all-gather.18
  685.9 102.8 reduce-scatter.3
  983.1 59.9 reduce-scatter.7
  1047.4 60.5 reduce-scatter.5
  1382.9 91.5 all-reduce.48
where the time goes:
time: 1500 us; the launch traced here: 1490 us
  matrix products  591 us (39%)
  local copies, waits for them, and re-layouts  424 us (28%)
  waiting for transfers between devices  313 us (21%)
  other arithmetic  141 us (9%)
  between operations  16 us (1%)
    conv_general_dilated x8, matrix products, convolve(): lax.conv_general_dilated(padded, kernel, (1, 1), 'VALID', precision=lax.P...  591 us
    unnamed x164, local copies, waits for them, and re-layouts  127 us
    psum x1, waiting for transfers between devices, local(): lax.psum((grad_first, grad_second, grad_coarse), ('face', 'tile'))  91.7 us
    all_gather x2, waiting for transfers between devices, fine_gather(): lax.all_gather(borders, ('face', 'tile'), axis=0, tiled=True)  90.1 us
    all_gather x2, waiting for transfers between devices, fine_gather(): lax.all_gather(columns, ('face', 'tile'), axis=0, tiled=True)  67.9 us
    all_gather x1, waiting for transfers between devices, local(): lax.all_gather(coarse[None], ('face', 'tile'), axis=0, tiled=True)  63.4 us
    mul x18, local copies, waits for them, and re-layouts, activate(): return jax.nn.gelu(values, approximate=False)  61.8 us
    concatenate x3, other arithmetic, assemble(): jnp.concatenate([top_row[:, :, None], middle, bottom[:, :, None]], axis=2)  56.6 us
  transfers between devices with their start and end apart: 9, of which 6 were waited for; matrix products, arithmetic and copies ran while one was open for 24% of the time, Pallas kernels for 0%

commit v1 on v0

--- a/solution.py
+++ b/solution.py
@@ -10,7 +10,7 @@
 
 def convolve(padded, kernel):
     return lax.conv_general_dilated(
-        padded, kernel, (1, 1), "VALID", precision=lax.Precision.HIGHEST
+        padded, kernel, (1, 1), "VALID", precision=lax.Precision.HIGH
     )
 
 
@@ -26,18 +26,24 @@
     return (columns, borders)
 
 
-def whole_pieces(gathered):
-    columns = jnp.stack([gathered[..., 0], gathered[..., -1]], axis=2)
-    borders = jnp.stack([gathered[..., 0, :], gathered[..., -1, :]], axis=2)
-    return (columns, borders)
-
-
 def fine_gather(tile_field):
     columns, borders = rim_pieces(tile_field)
-    return (
-        lax.all_gather(columns, ("face", "tile"), axis=0, tiled=True),
-        lax.all_gather(borders, ("face", "tile"), axis=0, tiled=True),
-    )
+    tile_rows = columns.shape[-1]
+    both = lax.all_gather(
+        jnp.concatenate([columns, borders], axis=-1), ("face", "tile"), axis=0, tiled=True
+    )
+    return (both[..., :tile_rows], both[..., tile_rows:])
+
+
+def fine_return(grad_columns, grad_borders):
+    tile_rows = grad_columns.shape[-1]
+    both = lax.psum_scatter(
+        jnp.concatenate([grad_columns, grad_borders], axis=-1),
+        ("face", "tile"),
+        scatter_dimension=0,
+        tiled=True,
+    )
+    return (both[..., :tile_rows], both[..., tile_rows:])
 
 
 def fetch_lines(
@@ -177,13 +183,8 @@
     coarse = features.reshape(
         slots_dev, channels, tile_rows // BLOCK, BLOCK, length // BLOCK, BLOCK
     ).mean(axis=(3, 5))
-    everything = lax.all_gather(coarse[None], ("face", "tile"), axis=0, tiled=True)
-
-    def coarse_frame(tile_field, gathered):
-        columns_all, borders_all = whole_pieces(gathered)
-        return framer(tile_field, columns_all, borders_all)
-
-    padded_low, low_pull = jax.vjp(coarse_frame, coarse, everything)
+    columns_low, borders_low = fine_gather(coarse)
+    padded_low, low_pull = jax.vjp(framer, coarse, columns_low, borders_low)
     coarse_act, coarse_pull = jax.vjp(convolve, padded_low, coarse_kernel)
     bottleneck, bottleneck_pull = jax.vjp(activate, coarse_act)
     widened = jnp.repeat(jnp.repeat(bottleneck, BLOCK, axis=2), BLOCK, axis=3)
@@ -194,20 +195,18 @@
     ).sum(axis=(3, 5))
     (grad_coarse_act,) = bottleneck_pull(grad_bottleneck)
     grad_padded_low, grad_coarse = coarse_pull(grad_coarse_act)
-    grad_local, grad_everything = low_pull(grad_padded_low)
-    returned = lax.psum_scatter(grad_everything, ("face", "tile"), scatter_dimension=0, tiled=True)
-    grad_low = grad_local + returned[0]
+    grad_local, grad_columns_low, grad_borders_low = low_pull(grad_padded_low)
+    back_low = fine_return(grad_columns_low, grad_borders_low)
+    (spread_low,) = jax.vjp(rim_pieces, coarse)[1](back_low)
+    grad_low = grad_local + spread_low
     grad_features = masked + jnp.repeat(jnp.repeat(grad_low, BLOCK, axis=2), BLOCK, axis=3) / (
         BLOCK * BLOCK
     )
     (grad_second_act,) = features_pull(grad_features)
     grad_padded_mid, grad_second = second_pull(grad_second_act)
     grad_hidden_local, grad_columns_mid, grad_borders_mid = frame_pull(grad_padded_mid)
-    back_columns_mid, back_borders_mid = (
-        lax.psum_scatter(grad_columns_mid, ("face", "tile"), scatter_dimension=0, tiled=True),
-        lax.psum_scatter(grad_borders_mid, ("face", "tile"), scatter_dimension=0, tiled=True),
-    )
-    (spread_mid,) = jax.vjp(rim_pieces, hidden)[1]((back_columns_mid, back_borders_mid))
+    back_mid = fine_return(grad_columns_mid, grad_borders_mid)
+    (spread_mid,) = jax.vjp(rim_pieces, hidden)[1](back_mid)
     grad_hidden = grad_hidden_local + spread_mid
     (grad_first_act,) = hidden_pull(grad_hidden)
     (grad_first,) = jax.vjp(partial(convolve, padded_in), first_kernel)[1](grad_first_act)

time: 1500 us -> 1120 us (0.75)
  matrix products: 591 us -> 332 us
  waiting for transfers between devices: 313 us -> 168 us
  blocking collectives: 0 us -> 24.6 us
    conv_general_dilated x8, matrix products: 591 us -> 332 us  [convolve(): lax.conv_general_dilated(padded, kernel, (1, 1), 'VALID', precision=lax.P...]
    all_gather x5 -> x2, waiting for transfers between devices: 221 us -> 42.2 us  [fine_gather(): lax.all_gather(jnp.concatenate([columns, borders], axis=-1), ('face', 'ti...]
    reduce_scatter x3 -> x2, waiting for transfers between devices: 0.02 us -> 33.1 us  [fine_return(): lax.psum_scatter(jnp.concatenate([grad_columns, grad_borders], axis=-1),...]
    all_gather x0 -> x1, blocking collectives: none -> 24.6 us  [fine_gather(): lax.all_gather(jnp.concatenate([columns, borders], axis=-1), ('face', 'ti...]
    unnamed x164 -> x151, local copies, waits for them, and re-layouts: 127 us -> 129 us
  transfers between devices with their start and end apart: 9 -> 5, of which waited for: 6 -> 3; matrix products, arithmetic and copies ran while one was open for 24% -> 17% of each run, Pallas kernels for 0% -> 0%
where the time goes in v1:
time: 1120 us; the launch traced here: 1110 us
  local copies, waits for them, and re-layouts  428 us (38%)
  matrix products  332 us (30%)
  waiting for transfers between devices  168 us (15%)
  other arithmetic  141 us (13%)
  blocking collectives  24.6 us (2%)
  between operations  16.1 us (1%)
    conv_general_dilated x8, matrix products, convolve(): lax.conv_general_dilated(padded, kernel, (1, 1), 'VALID', precision=lax.P...  332 us
    unnamed x151, local copies, waits for them, and re-layouts  129 us
    psum x1, waiting for transfers between devices, local(): lax.psum((grad_first, grad_second, grad_coarse), ('face', 'tile'))  92.4 us
    mul x18, local copies, waits for them, and re-layouts, activate(): return jax.nn.gelu(values, approximate=False)  60.4 us
    concatenate x3, other arithmetic, assemble(): jnp.concatenate([top_row[:, :, None], middle, bottom[:, :, None]], axis=2)  56.6 us
    another operation x12, local copies, waits for them, and re-layouts, activate(): return jax.nn.gelu(values, approximate=False)  45.2 us
    all_gather x2, waiting for transfers between devices, fine_gather(): lax.all_gather(jnp.concatenate([columns, borders], axis=-1), ('face', 'ti...  42.2 us
    conv_general_dilated x23, local copies, waits for them, and re-layouts, convolve(): lax.conv_general_dilated(padded, kernel, (1, 1), 'VALID', precision=lax.P...  33.6 us
  transfers between devices with their start and end apart: 5, of which 3 were waited for; matrix products, arithmetic and copies ran while one was open for 17% of the time, Pallas kernels for 0%

profile of v1, /device:TPU:0, one launch (start us, length us, event | category | flops | bytes accessed | tf_op | source)
XLA Modules:
  0.0 1109.9 jit_solution(18034019148153461933)
XLA Ops:
  34.8 42.2 %all-gather.3.cloned.1.call-done = f32[16,2,2,64,192]{4,3,2,1,0:T(8,128)} async-done(((f32[1,2,2,64,192]{4,3,2,1,0:T(8,128)}), f32[16,2,2,64,192]{4,3,2,1,0:T(8,128)}) %all-gather.3.cloned.1.call-update) | async-done | bytes 3145744 | tf_op jit(solution)/shard_map/all_gather | solution.py:32
  91.8 28.1 %fusion.199 = f32[64,66,2,130]{0,2,3,1:T(2,128)S(1)} fusion(f32[2,64,1,130]{1,0,3,2:T(2,128)S(1)} %maximum_bitcast_fusion.2, f32[2,64,64,1]{1,0,3,2:T(2,128)S(1)} %slice_bitcast_fusion.17, f32[2,64,64,128]{1,0,3,2:T(2,128)} %copy.858, f32[2,64,64,1]{1,0,3,2:T(2,128)S(1)} %slice_bitcast_fusion.18, f32[2,64,1,130]{1,0,3,2:T(2,128)S(1)} %maximum_bitcast_fusion.1), kind=kLoop, calls=%fused_computation.483 | loop fusion | flops 4392960 | bytes 8785920 | tf_op jit(solution)/shard_map/concatenate | solution.py:117
  124.5 54.7 %select_multiply_fusion.1 = (f32[64,16,17,64]{3,1,2,0:T(8,128)}, f32[64,16,17,64]{3,1,2,0:T(8,128)}, f32[64,16,17,64]{3,1,2,0:T(8,128)S(1)}, f32[64,16,17,64]{3,1,2,0:T(8,128)}) fusion(pred[16,17]{0,1:T(8,128)(4,1)S(1)} %copy-done.59, f32[64,64,3,3]{1,0,3,2:T(8,128)S(1)} %copy-done.56, f32[64,66,2,7,2]{0,3,2,4,1:T(8,128)S(1)} %slice.522, ...), kind=kOutput, calls=%fused_computation.65 | convolution fusion | flops 3926640640 | bytes 23042320 | tf_op jit(solution)/shard_map/conv_general_dilated | solution.py:12
  190.8 9.7 copy.1068
  285.8 28.1 %fusion.198 = f32[64,66,2,130]{0,2,3,1:T(2,128)S(1)} fusion(f32[2,64,1,130]{1,0,3,2:T(2,128)S(1)} %maximum_bitcast_fusion.4, f32[2,64,64,1]{1,0,3,2:T(2,128)S(1)} %slice_bitcast_fusion.13, f32[2,64,64,128]{1,0,3,2:T(2,128)} %bitcast.496, f32[2,64,64,1]{1,0,3,2:T(2,128)S(1)} %slice_bitcast_fusion.14, f32[2,64,1,130]{1,0,3,2:T(2,128)S(1)} %maximum_bitcast_fusion.3), kind=kLoop, calls=%fused_computation.482 | loop fusion | flops 4392960 | bytes 8785920 | tf_op jit(solution)/shard_map/jvp()/concatenate | solution.py:117
  318.3 54.7 %select_multiply_fusion = (f32[64,16,17,64]{3,1,2,0:T(8,128)}, f32[64,16,17,64]{3,1,2,0:T(8,128)}, f32[64,16,17,64]{3,1,2,0:T(8,128)S(1)}, f32[64,16,17,64]{3,1,2,0:T(8,128)}) fusion(pred[16,17]{0,1:T(8,128)(4,1)S(1)} %copy-done.59, f32[64,64,3,3]{1,0,3,2:T(8,128)S(1)} %copy-done, f32[64,66,2,7,2]{0,3,2,4,1:T(8,128)S(1)} %slice.554, ...), kind=kOutput, calls=%fused_computation.64 | convolution fusion | flops 3926640640 | bytes 23042320 | tf_op jit(solution)/shard_map/jvp()/conv_general_dilated | solution.py:12
  379.2 12.1 %fusion.170 = (f32[64,2,128,64]{3,0,2,1:T(8,128)}, f32[2,64,64,128]{1,2,3,0:T(8,128)}) fusion(f32[64,2,136,64]{3,0,2,1:T(8,128)} %bitcast.498), kind=kLoop, calls=%fused_computation.463 | loop fusion | bytes 12582912 | tf_op jit(solution)/shard_map/jvp()/mul | solution.py:18
  391.3 11.5 %copy.884 = f32[2,64,64,128]{1,3,2,0:T(8,128)} copy(f32[2,64,64,128]{1,2,3,0:T(8,128)} %get-tuple-element.72) | data formatting | bytes 8388608 | tf_op jit(solution)/shard_map/jvp()/mul | solution.py:18
  410.0 24.6 %all_gather.11 = f32[16,2,2,64,48]{3,4,2,1,0:T(8,128)S(1)} all-gather(f32[1,2,2,64,48]{3,4,2,1,0:T(8,128)S(1)} %pad_maximum_fusion.7), channel_id=1, replica_groups=mesh['groups'=2,'face'=8,'tile'=2] {'face','tile'}, dimensions={0}, use_global_device_ids=true | all-gather | bytes 835584 | tf_op jit(solution)/shard_map/all_gather | solution.py:32
  470.9 10.5 broadcast_multiply_fusion
  509.7 9.0 copy.989
  555.7 9.4 copy.998
  570.1 33.1 %reduce-scatter.3.cloned.1.call-done = f32[1,2,2,64,48]{3,4,2,1,0:T(8,128)} async-done(((f32[16,2,2,64,48]{3,4,2,1,0:T(8,128)}), f32[1,2,2,64,48]{3,4,2,1,0:T(8,128)}) %reduce-scatter.3.cloned.1.call-update) | async-done | bytes 49168 | tf_op jit(solution)/shard_map/reduce_scatter | solution.py:40
  622.0 12.3 %fusion.35 = f32[2,64,64,128]{3,2,1,0:T(8,128)} fusion(f32[64,2,128,64]{2,0,3,1:T(8,128)} %copy.998, f32[64,2,128,64]{2,0,3,1:T(8,128)} %copy.997, f32[64,2,128,64]{2,0,3,1:T(8,128)} %copy.989, f32[2,64,64,128]{3,2,1,0:T(8,128)} %get-tuple-element.202, f32[2,64,64,128]{3,2,1,0:T(8,128)} %copy.934), kind=kLoop, calls=%fused_computation.86 | loop fusion | flops 9437184 | bytes 25165824 | tf_op jit(solution)/shard_map/transpose(jvp())/add_any | solution.py:18
  634.3 9.3 copy.1007
  651.5 9.7 select_maximum_fusion.2
  661.2 11.3 %copy.940 = f32[64,64,2,8,19]{0,3,2,4,1:T(8,128)} copy(f32[64,64,2,8,19]{1,0,4,3,2:T(8,128)} %select_maximum_fusion.2) | data formatting | bytes 9961472 | tf_op jit(solution)/shard_map/transpose(jvp())/conv_general_dilated | solution.py:12
  672.4 24.5 %broadcast_select_fusion = f32[66,16,17,64]{3,1,2,0:T(8,128)S(1)} fusion(pred[16,17]{0,1:T(8,128)(4,1)S(1)} %copy-done.58, f32[64,64,3,3]{1,0,3,2:T(8,128)S(1)} %copy-done, f32[64,64,2,8,19]{0,3,2,4,1:T(8,128)} %copy.940), kind=kOutput, calls=%fused_computation.72 | convolution fusion | flops 3851520000 | bytes 9724176 | tf_op jit(solution)/shard_map/transpose(jvp())/conv_general_dilated | solution.py:12
  700.6 11.3 %copy.941 = f32[66,16,17,64]{0,3,2,1:T(8,128)} copy(f32[66,16,17,64]{3,1,2,0:T(8,128)} %copy-done.5) | data formatting | bytes 9191424 | tf_op jit(solution)/shard_map/transpose(jvp())/conv_general_dilated | solution.py:12
  741.2 11.2 %copy.999 = f32[66,2,130,64]{2,0,3,1:T(8,128)} copy(f32[66,2,130,64]{0,3,2,1:T(8,128)} %slice.603) | data formatting | bytes 8785920
  789.5 93.0 %fusion.187 = f32[64,64,3,3]{0,1,3,2:T(8,128)} fusion(f32[2,64,64,128]{1,0,3,2:T(2,128)} %copy.965, f32[2,64,1,130]{1,0,3,2:T(2,128)S(1)} %copy-done.18, f32[2,64,64,1]{1,0,3,2:T(2,128)S(1)} %copy-done.30, f32[2,64,64,128]{1,0,3,2:T(2,128)} %bitcast.497, f32[2,64,64,1]{1,0,3,2:T(2,128)S(1)} %copy-done.28, f32[2,64,1,130]{1,0,3,2:T(2,128)S(1)} %copy-done.16), kind=kOutput, calls=%fused_computation.480 | convolution fusion | flops 3628271616 | bytes 8734720 | tf_op jit(solution)/shard_map/transpose(jvp())/conv_general_dilated | solution.py:12
  890.1 13.4 %fusion.31 = f32[2,64,64,128]{3,2,1,0:T(8,128)} fusion(f32[64,2,128,64]{2,0,3,1:T(8,128)} %copy.1005, f32[64,2,128,64]{2,0,3,1:T(8,128)} %copy.1004, f32[64,2,128,64]{2,0,3,1:T(8,128)} %copy.988, f32[2,64,1,128]{3,2,1,0:T(1,128)S(1)} %bitcast.574, f32[2,64,66,130]{3,2,1,0:T(8,128)} %bitcast.488, f32[2,64,64,1]{3,2,1,0:T(8,128)} %copy.959, ...), kind=kLoop, calls=%fused_computation.80 | loop fusion | flops 12582912 | bytes 21168128 | tf_op jit(solution)/shard_map/transpose(jvp())/add_any | solution.py:18
  912.1 92.9 %fusion.186 = f32[64,64,3,3]{0,1,3,2:T(8,128)} fusion(f32[2,64,64,128]{1,0,3,2:T(2,128)} %copy.964, f32[2,64,1,130]{1,0,3,2:T(2,128)S(1)} %copy-done.14, f32[2,64,64,1]{1,0,3,2:T(2,128)S(1)} %copy-done.26, f32[2,64,64,128]{1,0,3,2:T(2,128)} %copy.858, f32[2,64,64,1]{1,0,3,2:T(2,128)S(1)} %copy-done.24, f32[2,64,1,130]{1,0,3,2:T(2,128)S(1)} %copy-done.12), kind=kOutput, calls=%fused_computation.479 | convolution fusion | flops 3628271616 | bytes 8734720 | tf_op jit(solution)/shard_map/transpose(jvp())/conv_general_dilated | solution.py:12
  1005.0 92.4 %all-reduce.49.cloned.1.call-done = (f32[64,64,3,3]{0,1,3,2:T(8,128)}, f32[64,64,3,3]{0,1,3,2:T(8,128)}, f32[64,64,3,3]{0,1,3,2:T(8,128)}) async-done(((f32[64,64,3,3]{0,1,3,2:T(8,128)}, f32[64,64,3,3]{0,1,3,2:T(8,128)}, f32[64,64,3,3]{0,1,3,2:T(8,128)}), (f32[64,64,3,3]{0,1,3,2:T(8,128)}, f32[64,64,3,3]{0,1,3,2:T(8,128)}, f32[64,64,3,3]{0,1,3,2:T(8,128)})) %all-reduce.49.cloned.1.call-update) | async-done | bytes 442384 | tf_op jit(solution)/shard_map/psum | solution.py:213
  (407 shorter events, 384.4 us)
Async XLA Ops:
  7.2 311.1 %copy-start = (f32[64,64,3,3]{1,0,3,2:T(8,128)S(1)}, f32[64,64,3,3]{1,0,3,2:T(8,128)}, u32[]{:S(2)}) copy-start(f32[64,64,3,3]{1,0,3,2:T(8,128)} %param.11) | copy-start | bytes 442372
  7.2 69.8 %all-gather.3.cloned.1.call-start = ((), (), s32[]{:S(2)}) async-start(), calls=%async_computation.2 | async-start | bytes 4456448 | tf_op jit(solution)/shard_map/all_gather | solution.py:32
  23.6 245.7 %all-gather.5.cloned.1.call-start = ((), (), s32[]{:S(2)}) async-start(), calls=%async_computation.3 | async-start | bytes 4456448 | tf_op jit(solution)/shard_map/all_gather | solution.py:32
  33.0 56.9 %copy-start.46 = (pred[2,4]{0,1:T(4,128)(4,1)}, pred[2,4]{0,1:T(4,128)(4,1)S(1)}, u32[]{:S(2)}) copy-start(pred[2,4]{0,1:T(4,128)(4,1)S(1)} %copy.850) | copy-start | bytes 28
  34.1 55.9 %copy-start.48 = (pred[2,4,1]{0,1,2:T(4,128)(4,1)}, pred[2,4,1]{0,1,2:T(4,128)(4,1)S(1)}, u32[]{:S(2)}) copy-start(pred[2,4,1]{0,1,2:T(4,128)(4,1)S(1)} %copy.971) | copy-start | bytes 28
  34.4 44.9 %copy-start.19 = (s32[8]{0:T(128)}, s32[8]{0:T(128)S(1)}, u32[]{:S(2)}) copy-start(s32[8]{0:T(128)S(1)} %reshape.649) | copy-start | bytes 100
  34.5 55.4 %copy-start.21 = (s32[8]{0:T(128)}, s32[8]{0:T(128)S(1)}, u32[]{:S(2)}) copy-start(s32[8]{0:T(128)S(1)} %reshape.655) | copy-start | bytes 100
  34.8 55.1 %copy-start.37 = (s32[8]{0:T(128)}, s32[8]{0:T(128)S(1)}, u32[]{:S(2)}) copy-start(s32[8]{0:T(128)S(1)} %reshape.635) | copy-start | bytes 100
  90.2 29.8 %copy-start.23 = (f32[2,64,64,1]{1,0,3,2:T(2,128)}, f32[2,64,64,1]{1,0,3,2:T(2,128)S(1)}, u32[]{:S(2)}) copy-start(f32[2,64,64,1]{1,0,3,2:T(2,128)S(1)} %slice_bitcast_fusion.18) | copy-start | bytes 98308
  90.3 29.7 %copy-start.25 = (f32[2,64,64,1]{1,0,3,2:T(2,128)}, f32[2,64,64,1]{1,0,3,2:T(2,128)S(1)}, u32[]{:S(2)}) copy-start(f32[2,64,64,1]{1,0,3,2:T(2,128)S(1)} %slice_bitcast_fusion.17) | copy-start | bytes 98308
  91.7 28.3 %copy-start.11 = (f32[2,64,1,130]{1,0,3,2:T(2,128)}, f32[2,64,1,130]{1,0,3,2:T(2,128)S(1)}, u32[]{:S(2)}) copy-start(f32[2,64,1,130]{1,0,3,2:T(2,128)S(1)} %maximum_bitcast_fusion.1) | copy-start | bytes 199684
  91.8 31.8 %copy-start.13 = (f32[2,64,1,130]{1,0,3,2:T(2,128)}, f32[2,64,1,130]{1,0,3,2:T(2,128)S(1)}, u32[]{:S(2)}) copy-start(f32[2,64,1,130]{1,0,3,2:T(2,128)S(1)} %maximum_bitcast_fusion.2) | copy-start | bytes 199684
  205.1 398.0 %reduce-scatter.3.cloned.1.call-start = ((), (), s32[]{:S(2)}) async-start(), calls=%async_computation.4 | async-start | bytes 1671168 | tf_op jit(solution)/shard_map/reduce_scatter | solution.py:40
  260.3 17.7 %copy-start.22 = (s32[8]{0:T(128)S(1)}, s32[8]{0:T(128)}, u32[]{:S(2)}) copy-start(s32[8]{0:T(128)} %copy-done.21) | copy-start | bytes 100
  284.2 29.7 %copy-start.27 = (f32[2,64,64,1]{1,0,3,2:T(2,128)}, f32[2,64,64,1]{1,0,3,2:T(2,128)S(1)}, u32[]{:S(2)}) copy-start(f32[2,64,64,1]{1,0,3,2:T(2,128)S(1)} %slice_bitcast_fusion.14) | copy-start | bytes 98308
  284.3 29.6 %copy-start.29 = (f32[2,64,64,1]{1,0,3,2:T(2,128)}, f32[2,64,64,1]{1,0,3,2:T(2,128)S(1)}, u32[]{:S(2)}) copy-start(f32[2,64,64,1]{1,0,3,2:T(2,128)S(1)} %slice_bitcast_fusion.13) | copy-start | bytes 98308
  285.6 28.3 %copy-start.15 = (f32[2,64,1,130]{1,0,3,2:T(2,128)}, f32[2,64,1,130]{1,0,3,2:T(2,128)S(1)}, u32[]{:S(2)}) copy-start(f32[2,64,1,130]{1,0,3,2:T(2,128)S(1)} %maximum_bitcast_fusion.3) | copy-start | bytes 199684
  285.7 31.8 %copy-start.17 = (f32[2,64,1,130]{1,0,3,2:T(2,128)}, f32[2,64,1,130]{1,0,3,2:T(2,128)S(1)}, u32[]{:S(2)}) copy-start(f32[2,64,1,130]{1,0,3,2:T(2,128)S(1)} %maximum_bitcast_fusion.4) | copy-start | bytes 199684
  402.8 33.1 %copy-start.45 = (s32[8]{0:T(128)S(1)}, s32[8]{0:T(128)}, u32[]{:S(2)}) copy-start(s32[8]{0:T(128)} %reshape.679) | copy-start | bytes 100
  545.0 337.5 %reduce-scatter.5.cloned.1.call-start = ((), (), s32[]{:S(2)}) async-start(), calls=%async_computation.5 | async-start | bytes 4456448 | tf_op jit(solution)/shard_map/reduce_scatter | solution.py:40
  752.4 18.1 %copy-start.54 = (pred[66]{0:T(512)(128)(4,1)S(1)}, pred[66]{0:T(512)(128)(4,1)}, u32[]{:S(2)}) copy-start(pred[66]{0:T(512)(128)(4,1)} %constant.232.clone.1) | copy-start | bytes 202
  752.4 18.3 %copy-start.51 = (pred[2,4,1]{0,1,2:T(4,128)(4,1)S(1)}, pred[2,4,1]{0,1,2:T(4,128)(4,1)}, u32[]{:S(2)}) copy-start(pred[2,4,1]{0,1,2:T(4,128)(4,1)} %copy-done.48) | copy-start | bytes 28
  789.4 308.1 %all-reduce.49.cloned.1.call-start = ((), (), s32[]{:S(2)}) async-start(), calls=%async_computation.6 | async-start | bytes 1769472 | tf_op jit(solution)/shard_map/psum | solution.py:213
  912.1 190.9 %copy-start.1 = (f32[64,64,3,3]{1,0,3,2:T(8,128)S(1)}, f32[64,64,3,3]{1,0,3,2:T(8,128)}, u32[]{:S(2)}) copy-start(f32[64,64,3,3]{1,0,3,2:T(8,128)} %param.11) | copy-start | bytes 442372
  (43 other events, 391.1 us)
Sparse Core Ops, SparseCore 0:
  23.7 53.2 all-gather.2
  205.3 49.0 all-gather.4
  545.2 57.9 reduce-scatter.2
  789.5 71.7 reduce-scatter.4
  1005.2 92.2 all-reduce.48

commit v2 on v1

--- a/solution.py
+++ b/solution.py
@@ -16,6 +16,18 @@
 
 def activate(values):
     return jax.nn.gelu(values, approximate=False)
+
+
+def activation_grad(values, grads):
+    return jax.vjp(activate, lax.optimization_barrier(values))[1](grads)[0]
+
+
+def split_sum(values, devices):
+    turned = values.transpose(2, 3, 1, 0)
+    shares = turned.reshape(devices, -1, 128)
+    share = lax.psum_scatter(shares, ("face", "tile"), scatter_dimension=0, tiled=True)
+    whole = lax.all_gather(share, ("face", "tile"), axis=0, tiled=True)
+    return whole.reshape(turned.shape).transpose(3, 2, 0, 1)
 
 
 def rim_pieces(tile_field):
@@ -172,11 +184,11 @@
     columns_in, borders_in = fine_gather(fields)
     padded_in = framer(fields, columns_in, borders_in)
     first_act = convolve(padded_in, first_kernel)
-    hidden, hidden_pull = jax.vjp(activate, first_act)
+    hidden = activate(first_act)
     columns_mid, borders_mid = fine_gather(hidden)
     padded_mid, frame_pull = jax.vjp(framer, hidden, columns_mid, borders_mid)
     second_act, second_pull = jax.vjp(convolve, padded_mid, second_kernel)
-    features, features_pull = jax.vjp(activate, second_act)
+    features = activate(second_act)
     channels = features.shape[1]
     tile_rows = features.shape[2]
     length = features.shape[3]
@@ -202,17 +214,17 @@
     grad_features = masked + jnp.repeat(jnp.repeat(grad_low, BLOCK, axis=2), BLOCK, axis=3) / (
         BLOCK * BLOCK
     )
-    (grad_second_act,) = features_pull(grad_features)
+    grad_second_act = activation_grad(second_act, grad_features)
     grad_padded_mid, grad_second = second_pull(grad_second_act)
     grad_hidden_local, grad_columns_mid, grad_borders_mid = frame_pull(grad_padded_mid)
     back_mid = fine_return(grad_columns_mid, grad_borders_mid)
     (spread_mid,) = jax.vjp(rim_pieces, hidden)[1](back_mid)
     grad_hidden = grad_hidden_local + spread_mid
-    (grad_first_act,) = hidden_pull(grad_hidden)
+    grad_second, grad_hidden = lax.optimization_barrier((grad_second, grad_hidden))
+    grad_first_act = activation_grad(first_act, grad_hidden)
     (grad_first,) = jax.vjp(partial(convolve, padded_in), first_kernel)[1](grad_first_act)
-    grad_first, grad_second, grad_coarse = lax.psum(
-        (grad_first, grad_second, grad_coarse), ("face", "tile")
-    )
+    grad_second, grad_coarse = lax.psum((grad_second, grad_coarse), ("face", "tile"))
+    grad_first = split_sum(grad_first, face_count * tile_count)
     return (section_output, grad_first, grad_second, grad_coarse)
 
 

time: 1120 us -> 1070 us (0.955)
  local copies, waits for them, and re-layouts: 428 us -> 343 us
  matrix products: 332 us -> 358 us
  blocking collectives: 24.6 us -> 45.5 us
  waiting for transfers between devices: 168 us -> 151 us
    psum x1, waiting for transfers between devices: 92.4 us -> 0.02 us  [local(): lax.psum((grad_second, grad_coarse), ('face', 'tile'))]
    transpose x0 -> x1, matrix products: none -> 91.9 us  [split_sum(): turned = values.transpose(2, 3, 1, 0)]
    conv_general_dilated x8 -> x7, matrix products: 332 us -> 266 us  [convolve(): lax.conv_general_dilated(padded, kernel, (1, 1), 'VALID', precision=lax.P...]
    unnamed x5 -> x7, waiting for transfers between devices: 0.08 us -> 50.9 us
    another operation x12 -> x4, local copies, waits for them, and re-layouts: 45.2 us -> 0.5 us  [activate(): return jax.nn.gelu(values, approximate=False)]
    unnamed x151 -> x139, local copies, waits for them, and re-layouts: 129 us -> 90.9 us
    all_gather x2, waiting for transfers between devices: 42.2 us -> 68 us  [fine_gather(): lax.all_gather(jnp.concatenate([columns, borders], axis=-1), ('face', 'ti...]
    conv_general_dilated x23 -> x27, local copies, waits for them, and re-layouts: 33.6 us -> 56 us  [convolve(): lax.conv_general_dilated(padded, kernel, (1, 1), 'VALID', precision=lax.P...]
  transfers between devices with their start and end apart: 5 -> 6, of which waited for: 3 -> 4; matrix products, arithmetic and copies ran while one was open for 17% -> 24% of each run, Pallas kernels for 0% -> 0%
where the time goes in v2:
time: 1070 us; the launch traced here: 1060 us
  matrix products  358 us (33%)
  local copies, waits for them, and re-layouts  343 us (32%)
  waiting for transfers between devices  151 us (14%)
  other arithmetic  144 us (13%)
  blocking collectives  45.5 us (4%)
  between operations  16.2 us (2%)
    conv_general_dilated x7, matrix products, convolve(): lax.conv_general_dilated(padded, kernel, (1, 1), 'VALID', precision=lax.P...  266 us
    transpose x1, matrix products, split_sum(): turned = values.transpose(2, 3, 1, 0)  91.9 us
    unnamed x139, local copies, waits for them, and re-layouts  90.9 us
    all_gather x2, waiting for transfers between devices, fine_gather(): lax.all_gather(jnp.concatenate([columns, borders], axis=-1), ('face', 'ti...  68 us
    concatenate x3, other arithmetic, assemble(): jnp.concatenate([top_row[:, :, None], middle, bottom[:, :, None]], axis=2)  56.6 us
    conv_general_dilated x27, local copies, waits for them, and re-layouts, convolve(): lax.conv_general_dilated(padded, kernel, (1, 1), 'VALID', precision=lax.P...  56 us
    unnamed x7, waiting for transfers between devices  50.9 us
    mul x14, local copies, waits for them, and re-layouts, activate(): return jax.nn.gelu(values, approximate=False)  39 us
  transfers between devices with their start and end apart: 6, of which 4 were waited for; matrix products, arithmetic and copies ran while one was open for 24% of the time, Pallas kernels for 0%

profile of v2, /device:TPU:0, one launch (start us, length us, event | category | flops | bytes accessed | tf_op | source)
XLA Modules:
  0.0 1057.5 jit_solution(6484097872183846274)
XLA Ops:
  34.7 42.5 %all-gather.3.cloned.1.call-done = f32[16,2,2,64,192]{4,3,2,1,0:T(8,128)} async-done(((f32[1,2,2,64,192]{4,3,2,1,0:T(8,128)}), f32[16,2,2,64,192]{4,3,2,1,0:T(8,128)}) %all-gather.3.cloned.1.call-update) | async-done | bytes 3145744 | tf_op jit(solution)/shard_map/all_gather | solution.py:44
  91.8 28.1 %fusion.217 = f32[64,66,2,130]{0,2,3,1:T(2,128)S(1)} fusion(f32[2,64,1,130]{1,0,3,2:T(2,128)S(1)} %maximum_bitcast_fusion.2, f32[2,64,64,1]{1,0,3,2:T(2,128)S(1)} %slice_bitcast_fusion.17, f32[2,64,64,128]{1,0,3,2:T(2,128)} %copy.804, f32[2,64,64,1]{1,0,3,2:T(2,128)S(1)} %slice_bitcast_fusion.18, f32[2,64,1,130]{1,0,3,2:T(2,128)S(1)} %maximum_bitcast_fusion.1), kind=kLoop, calls=%fused_computation.508 | loop fusion | flops 4392960 | bytes 8785920 | tf_op jit(solution)/shard_map/concatenate | solution.py:129
  124.5 72.1 %fusion.13 = (f32[64,16,17,64]{3,1,2,0:T(8,128)S(1)}, f32[64,16,17,64]{3,1,2,0:T(8,128)}) fusion(f32[64,64,3,3]{1,0,3,2:T(8,128)S(1)} %copy-done.51, f32[64,66,2,7,2]{0,3,2,4,1:T(8,128)S(1)} %slice.518, f32[64,66,2,8,17]{0,3,2,4,1:T(8,128)S(1)} %copy.808, pred[16,17]{0,1:T(8,128)(4,1)S(1)} %copy-done.55), kind=kOutput, calls=%fused_computation.36 | convolution fusion | flops 3926640640 | bytes 14129424 | tf_op jit(solution)/shard_map/conv_general_dilated | solution.py:12
  208.6 9.7 copy.1001
  246.5 25.5 %all-gather.5.cloned.1.call-done = f32[16,2,2,64,192]{4,3,2,1,0:T(8,128)} async-done(((f32[1,2,2,64,192]{4,3,2,1,0:T(8,128)}), f32[16,2,2,64,192]{4,3,2,1,0:T(8,128)}) %all-gather.5.cloned.1.call-update) | async-done | bytes 3145744 | tf_op jit(solution)/shard_map/all_gather | solution.py:44
  285.8 28.1 %fusion.216 = f32[64,66,2,130]{0,2,3,1:T(2,128)S(1)} fusion(f32[2,64,1,130]{1,0,3,2:T(2,128)S(1)} %maximum_bitcast_fusion.4, f32[2,64,64,1]{1,0,3,2:T(2,128)S(1)} %slice_bitcast_fusion.13, f32[2,64,64,128]{1,0,3,2:T(2,128)} %bitcast.462, f32[2,64,64,1]{1,0,3,2:T(2,128)S(1)} %slice_bitcast_fusion.14, f32[2,64,1,130]{1,0,3,2:T(2,128)S(1)} %maximum_bitcast_fusion.3), kind=kLoop, calls=%fused_computation.507 | loop fusion | flops 4392960 | bytes 8785920 | tf_op jit(solution)/shard_map/jvp()/concatenate | solution.py:129
  318.4 63.1 %fusion.15 = (f32[64,16,17,64]{3,1,2,0:T(8,128)S(1)}, f32[64,16,17,64]{3,1,2,0:T(8,128)}) fusion(f32[64,64,3,3]{1,0,3,2:T(8,128)S(1)} %copy-done, f32[64,66,2,7,2]{0,3,2,4,1:T(8,128)S(1)} %slice.550, f32[64,66,2,8,17]{0,3,2,4,1:T(8,128)S(1)} %copy.827, pred[16,17]{0,1:T(8,128)(4,1)S(1)} %copy-done.55), kind=kOutput, calls=%fused_computation.38 | convolution fusion | flops 3926640640 | bytes 14129424 | tf_op jit(solution)/shard_map/jvp()/conv_general_dilated | solution.py:12
  387.7 12.2 %fusion.188 = (f32[64,2,128,64]{3,0,2,1:T(8,128)}, f32[2,64,64,128]{1,2,3,0:T(8,128)}) fusion(f32[64,2,136,64]{3,0,2,1:T(8,128)} %bitcast.464), kind=kLoop, calls=%fused_computation.488 | loop fusion | bytes 12582912 | tf_op jit(solution)/shard_map/mul | solution.py:18
  399.9 11.6 %copy.830 = f32[2,64,64,128]{1,3,2,0:T(8,128)} copy(f32[2,64,64,128]{1,2,3,0:T(8,128)} %get-tuple-element.63) | data formatting | bytes 8388608 | tf_op jit(solution)/shard_map/mul | solution.py:18
  418.6 25.3 %all_gather.14 = f32[16,2,2,64,48]{3,4,2,1,0:T(8,128)S(1)} all-gather(f32[1,2,2,64,48]{3,4,2,1,0:T(8,128)S(1)} %pad_maximum_fusion.7), channel_id=1, replica_groups=mesh['groups'=2,'face'=8,'tile'=2] {'face','tile'}, dimensions={0}, use_global_device_ids=true | all-gather | bytes 835584 | tf_op jit(solution)/shard_map/all_gather | solution.py:44
  479.1 10.5 broadcast_multiply_fusion
  538.9 32.1 %reduce-scatter.6.cloned.1.call-done = f32[1,2,2,64,48]{3,4,2,1,0:T(8,128)} async-done(((f32[16,2,2,64,48]{3,4,2,1,0:T(8,128)}), f32[1,2,2,64,48]{3,4,2,1,0:T(8,128)}) %reduce-scatter.6.cloned.1.call-update) | async-done | bytes 49168 | tf_op jit(solution)/shard_map/reduce_scatter | solution.py:52
  589.8 12.6 %fusion.39 = f32[2,64,64,128]{3,2,1,0:T(8,128)} fusion(f32[2,64,64,128]{3,2,1,0:T(8,128)} %get-tuple-element.193, f32[2,64,64,128]{3,2,1,0:T(8,128)} %copy.880, f32[2,64,64,128]{3,2,1,0:T(8,128)} %bitcast.474), kind=kLoop, calls=%fused_computation.84 | loop fusion | flops 75497472 | bytes 16777216 | tf_op jit(solution)/shard_map/transpose(jvp())/add_any | solution.py:18
  610.8 9.3 copy.941
  628.0 9.7 select_maximum_fusion.2
  637.7 11.3 %copy.883 = f32[64,64,2,8,19]{0,3,2,4,1:T(8,128)} copy(f32[64,64,2,8,19]{1,0,4,3,2:T(8,128)} %select_maximum_fusion.2) | data formatting | bytes 9961472 | tf_op jit(solution)/shard_map/transpose(jvp())/conv_general_dilated | solution.py:12
  649.0 25.5 %broadcast_select_fusion = f32[66,16,17,64]{3,1,2,0:T(8,128)} fusion(pred[16,17]{0,1:T(8,128)(4,1)S(1)} %copy-done.54, f32[64,64,3,3]{1,0,3,2:T(8,128)S(1)} %copy-done, f32[64,64,2,8,19]{0,3,2,4,1:T(8,128)} %copy.883), kind=kOutput, calls=%fused_computation.78 | convolution fusion | flops 3851520000 | bytes 9724176 | tf_op jit(solution)/shard_map/transpose(jvp())/conv_general_dilated | solution.py:12
  674.4 11.3 %copy.884 = f32[66,16,17,64]{0,3,2,1:T(8,128)} copy(f32[66,16,17,64]{3,1,2,0:T(8,128)} %broadcast_select_fusion) | data formatting | bytes 9191424 | tf_op jit(solution)/shard_map/transpose(jvp())/conv_general_dilated | solution.py:12
  695.3 11.4 %copy.935 = f32[66,2,130,64]{2,0,3,1:T(8,128)} copy(f32[66,2,130,64]{0,3,2,1:T(8,128)} %slice.597) | data formatting | bytes 8785920
  755.4 93.1 %fusion.204 = f32[64,64,3,3]{0,1,3,2:T(8,128)} fusion(f32[2,64,64,128]{1,0,3,2:T(2,128)} %copy.881, f32[2,64,1,130]{1,0,3,2:T(2,128)S(1)} %copy-done.17, f32[2,64,64,1]{1,0,3,2:T(2,128)S(1)} %copy-done.27, f32[2,64,64,128]{1,0,3,2:T(2,128)} %bitcast.463, f32[2,64,64,1]{1,0,3,2:T(2,128)S(1)} %copy-done.29, f32[2,64,1,130]{1,0,3,2:T(2,128)S(1)} %copy-done.19), kind=kOutput, calls=%fused_computation.504 | convolution fusion | flops 3628271616 | bytes 8734720 | tf_op jit(solution)/shard_map/transpose(jvp())/conv_general_dilated | solution.py:12
  862.7 10.7 %fusion.43 = f32[2,64,64,128]{3,2,1,0:T(8,128)} fusion(f32[2,64,64,128]{3,2,1,0:T(8,128)S(1)} %slice_add_fusion, f32[2,64,64,128]{3,2,1,0:T(8,128)S(1)} %bitcast.473), kind=kLoop, calls=%fused_computation.88 | loop fusion | flops 74448896 | bytes 12582912 | tf_op jit(solution)/shard_map/transpose(jvp())/add_any | solution.py:18
  882.1 91.9 %fusion.205 = f32[3,3,64,64]{3,2,1,0:T(8,128)S(1)} fusion(f32[2,64,64,128]{1,0,3,2:T(2,128)} %copy.903, f32[2,64,1,130]{1,0,3,2:T(2,128)S(1)} %copy-done.13, f32[2,64,64,1]{1,0,3,2:T(2,128)S(1)} %copy-done.23, f32[2,64,64,128]{1,0,3,2:T(2,128)} %copy.804, f32[2,64,64,1]{1,0,3,2:T(2,128)S(1)} %copy-done.25, f32[2,64,1,130]{1,0,3,2:T(2,128)S(1)} %copy-done.15), kind=kOutput, calls=%fused_computation.505 | convolution fusion | flops 3628271616 | bytes 8734720 | tf_op jit(solution)/shard_map/transpose | solution.py:26
  978.5 50.8 %reduce-scatter.10.cloned.1.call-done = f32[1,18,128]{2,1,0:T(8,128)} async-done(((f32[16,18,128]{2,1,0:T(8,128)}), f32[1,18,128]{2,1,0:T(8,128)}) %reduce-scatter.10.cloned.1.call-update) | async-done | bytes 9232
  1029.3 20.2 %all_gather.15 = f32[16,18,128]{2,1,0:T(8,128)S(1)} all-gather(f32[1,18,128]{2,1,0:T(8,128)} %reduce-scatter.10.cloned.1.call-done), channel_id=1, replica_groups=mesh['groups'=2,'face'=8,'tile'=2] {'face','tile'}, dimensions={0}, use_global_device_ids=true | all-gather | bytes 156672 | tf_op jit(solution)/shard_map/all_gather | solution.py:29
  (396 shorter events, 322.6 us)
Async XLA Ops:
  7.2 311.2 %copy-start = (f32[64,64,3,3]{1,0,3,2:T(8,128)S(1)}, f32[64,64,3,3]{1,0,3,2:T(8,128)}, u32[]{:S(2)}) copy-start(f32[64,64,3,3]{1,0,3,2:T(8,128)} %param.11) | copy-start | bytes 442372
  7.2 70.0 %all-gather.3.cloned.1.call-start = ((), (), s32[]{:S(2)}) async-start(), calls=%async_computation.3 | async-start | bytes 4456448 | tf_op jit(solution)/shard_map/all_gather | solution.py:44
  23.6 248.4 %all-gather.5.cloned.1.call-start = ((), (), s32[]{:S(2)}) async-start(), calls=%async_computation.4 | async-start | bytes 4456448 | tf_op jit(solution)/shard_map/all_gather | solution.py:44
  34.7 411.5 %copy-start.43 = (pred[2,4,1]{0,1,2:T(4,128)(4,1)}, pred[2,4,1]{0,1,2:T(4,128)(4,1)S(1)}, u32[]{:S(2)}) copy-start(pred[2,4,1]{0,1,2:T(4,128)(4,1)S(1)} %copy.909) | copy-start | bytes 28
  90.2 29.8 %copy-start.22 = (f32[2,64,64,1]{1,0,3,2:T(2,128)}, f32[2,64,64,1]{1,0,3,2:T(2,128)S(1)}, u32[]{:S(2)}) copy-start(f32[2,64,64,1]{1,0,3,2:T(2,128)S(1)} %slice_bitcast_fusion.17) | copy-start | bytes 98308
  90.3 29.7 %copy-start.24 = (f32[2,64,64,1]{1,0,3,2:T(2,128)}, f32[2,64,64,1]{1,0,3,2:T(2,128)S(1)}, u32[]{:S(2)}) copy-start(f32[2,64,64,1]{1,0,3,2:T(2,128)S(1)} %slice_bitcast_fusion.18) | copy-start | bytes 98308
  91.7 28.3 %copy-start.12 = (f32[2,64,1,130]{1,0,3,2:T(2,128)}, f32[2,64,1,130]{1,0,3,2:T(2,128)S(1)}, u32[]{:S(2)}) copy-start(f32[2,64,1,130]{1,0,3,2:T(2,128)S(1)} %maximum_bitcast_fusion.2) | copy-start | bytes 199684
  91.8 28.2 %copy-start.14 = (f32[2,64,1,130]{1,0,3,2:T(2,128)}, f32[2,64,1,130]{1,0,3,2:T(2,128)S(1)}, u32[]{:S(2)}) copy-start(f32[2,64,1,130]{1,0,3,2:T(2,128)S(1)} %maximum_bitcast_fusion.1) | copy-start | bytes 199684
  208.6 14.3 %copy-start.2 = (s32[16]{0:T(128)S(1)}, s32[16]{0:T(128)}, u32[]{:S(2)}) copy-start(s32[16]{0:T(128)} %param.13) | copy-start | bytes 196
  222.8 348.3 %reduce-scatter.6.cloned.1.call-start = ((), (), s32[]{:S(2)}) async-start(), calls=%async_computation.5 | async-start | bytes 1671168 | tf_op jit(solution)/shard_map/reduce_scatter | solution.py:52
  285.2 28.8 %copy-start.26 = (f32[2,64,64,1]{1,0,3,2:T(2,128)}, f32[2,64,64,1]{1,0,3,2:T(2,128)S(1)}, u32[]{:S(2)}) copy-start(f32[2,64,64,1]{1,0,3,2:T(2,128)S(1)} %slice_bitcast_fusion.13) | copy-start | bytes 98308
  285.3 28.7 %copy-start.28 = (f32[2,64,64,1]{1,0,3,2:T(2,128)}, f32[2,64,64,1]{1,0,3,2:T(2,128)S(1)}, u32[]{:S(2)}) copy-start(f32[2,64,64,1]{1,0,3,2:T(2,128)S(1)} %slice_bitcast_fusion.14) | copy-start | bytes 98308
  285.7 28.3 %copy-start.16 = (f32[2,64,1,130]{1,0,3,2:T(2,128)}, f32[2,64,1,130]{1,0,3,2:T(2,128)S(1)}, u32[]{:S(2)}) copy-start(f32[2,64,1,130]{1,0,3,2:T(2,128)S(1)} %maximum_bitcast_fusion.4) | copy-start | bytes 199684
  285.8 28.2 %copy-start.18 = (f32[2,64,1,130]{1,0,3,2:T(2,128)}, f32[2,64,1,130]{1,0,3,2:T(2,128)S(1)}, u32[]{:S(2)}) copy-start(f32[2,64,1,130]{1,0,3,2:T(2,128)S(1)} %maximum_bitcast_fusion.3) | copy-start | bytes 199684
  513.9 334.6 %reduce-scatter.8.cloned.1.call-start = ((), (), s32[]{:S(2)}) async-start(), calls=%async_computation.6 | async-start | bytes 4456448 | tf_op jit(solution)/shard_map/reduce_scatter | solution.py:52
  524.6 9.3 copy-start.32
  524.6 9.3 copy-start.34
  524.6 9.3 copy-start.38
  524.6 9.3 copy-start.40
  637.7 11.3 %copy-start.54 = (pred[16,17]{0,1:T(8,128)(4,1)S(1)}, pred[16,17]{0,1:T(8,128)(4,1)}, u32[]{:S(2)}) copy-start(pred[16,17]{0,1:T(8,128)(4,1)} %constant.351) | copy-start | bytes 820
  727.2 10.1 copy-start.45
  754.4 220.4 %all-reduce.50.cloned.1.call-start = ((), (), s32[]{:S(2)}) async-start(), calls=%async_computation.8 | async-start | bytes 1179648 | tf_op jit(solution)/shard_map/psum | solution.py:226
  882.0 147.3 %reduce-scatter.10.cloned.1.call-start = ((), (), s32[]{:S(2)}) async-start(), calls=%async_computation.7 | async-start | bytes 208896
  882.1 168.4 %copy-start.1 = (f32[64,64,3,3]{1,0,3,2:T(8,128)S(1)}, f32[64,64,3,3]{1,0,3,2:T(8,128)}, u32[]{:S(2)}) copy-start(f32[64,64,3,3]{1,0,3,2:T(8,128)} %param.11) | copy-start | bytes 442372
  (42 other events, 174.8 us)
Sparse Core Ops, SparseCore 0:
  23.7 53.4 all-gather.2
  222.9 49.0 all-gather.4
  514.0 56.9 reduce-scatter.5
  754.5 71.4 reduce-scatter.7
  882.1 90.6 all-reduce.49
  976.7 52.5 reduce-scatter.9
